TPU v7x, 32 devices: a whole 2x2x4 slice. The times are simulated.
32 devices in a mesh: groups: 2 (over x), bx: 16 (over z, y, core).
Axes of the slice: x: 2, y: 2, z: 4, core: 2. Of those that a mesh axis runs over, the one named last changes fastest.
Arguments:
- rhs: bfloat16 [192, 512, 256], P(('groups', 'bx')), parts along dimension 0, may hold values from -6 to 6
- tiles: bfloat16 [4, 3, 192, 256, 256], P(None, None, ('groups', 'bx')), parts along dimension 2, may hold values from -0.1875 to 0.1875
- occupancy: int32 [192, 256], P(('groups', 'bx')), parts along dimension 0, may hold values 0 or 1
Outputs:
- applied: float32 [192, 512, 256], P(('groups', 'bx')), parts along dimension 0
There are 2 independent parts, one for each index of `groups`. A program takes and returns all parts, laid end to end along the dimension named above; each array names one. Nothing has to cross between parts.
All inputs are finite; a program needn't handle non-finite values. No bound on the sum of `occupancy` on one device may be relied on, other than what follows from the above.
Results may differ from a plain program's by a relative error of at most 0.0026.
Values may be sent and summed in bfloat16 or wider, within the bound.
A program may use at most 64 MiB of HBM per device.

v0:
```python
import jax
import jax.numpy as jnp
from jax import lax
from jax.sharding import PartitionSpec as P

LEVELS = 3


def from_partner(x, axis, stride):
    return lax.ppermute(x, axis, [(i, i ^ 1 << stride) for i in range(lax.axis_size(axis))])


def passed_along(x, axis, by):
    count = lax.axis_size(axis)
    return lax.ppermute(x, axis, [(i, (i + by) % count) for i in range(count)])


def product(source, weight):
    return jnp.einsum("bnr,brs->bns", source, weight, preferred_element_type=jnp.float32)


def body(rhs, tiles, occupancy):
    state = rhs.astype(jnp.float32)
    keep = occupancy.astype(jnp.float32)[:, None, :]
    for level in range(LEVELS):
        sent = state.astype(jnp.bfloat16)
        partner = from_partner(sent, "bx", level)
        left = passed_along(sent, "bx", 1)
        right = passed_along(sent, "bx", -1)
        coupled = product(sent, tiles[0, level])
        coupled = coupled + product(partner, tiles[1, level])
        coupled = coupled + product(left, tiles[2, level])
        coupled = coupled + product(right, tiles[3, level])
        state = state + keep * coupled
    return state


def solution(mesh):
    placed = (
        P(("groups", "bx"), None, None),
        P(None, None, ("groups", "bx"), None, None),
        P(("groups", "bx"), None),
    )
    return jax.shard_map(
        body, mesh=mesh, in_specs=placed, out_specs=P(("groups", "bx"), None, None), check_vma=False
    )
```

profile of v0, /device:TPU:0, one launch (start us, length us, event | category | flops | bytes accessed | tf_op | source)
XLA Modules:
  0.0 181.8 jit_solution(11899199041847695552)
XLA Ops:
  0.0 0.5 collective-permute-start
  0.5 0.1 collective-permute-start.1
  0.5 5.6 %collective-permute-start.2 = (bf16[6,512,256]{2,1,0:T(8,128)(2,1)}, bf16[6,512,256]{2,1,0:T(8,128)(2,1)S(1)}, u32[]{:S(2)}, u32[]{:S(2)}) collective-permute-start(bf16[6,512,256]{2,1,0:T(8,128)(2,1)} %param.3), channel_id=1, source_target_pairs={{0,15},{1,0},{2,1},{3,2},{4,3},{5,4},{6,5},{7,6},{8,7},{9,8},{10,9... | collective-permute-start | bytes 4718600 | tf_op jit(solution)/shard_map/ppermute | solution.py:15
  6.1 0.7 convert_element_type.14
  6.8 0.0 copy-start
  6.8 2.3 %fusion.28 = f32[6,512,256]{2,1,0:T(8,128)S(1)} fusion(bf16[6,512,256]{2,1,0:T(8,128)(2,1)} %param.3, bf16[4,3,6,256,256]{4,3,2,1,0:T(8,128)(2,1)} %param.4), kind=kOutput, calls=%fused_computation.25 | convolution fusion | flops 402653184 | bytes 5505024 | tf_op jit(solution)/shard_map/bnr,brs->bns/dot_general | solution.py:19
  9.2 0.0 collective-permute-done
  9.2 2.2 %fusion.26 = f32[6,512,256]{2,1,0:T(8,128)S(1)} fusion(bf16[6,512,256]{2,1,0:T(8,128)(2,1)S(1)} %collective-permute-done, bf16[4,3,6,256,256]{4,3,2,1,0:T(8,128)(2,1)} %param.4), kind=kOutput, calls=%fused_computation.23 | convolution fusion | flops 402653184 | bytes 5505024 | tf_op jit(solution)/shard_map/bnr,brs->bns/dot_general | solution.py:19
  11.3 0.0 copy-start.1
  11.3 13.2 %collective-permute-done.1 = bf16[6,512,256]{2,1,0:T(8,128)(2,1)S(1)} collective-permute-done((bf16[6,512,256]{2,1,0:T(8,128)(2,1)}, bf16[6,512,256]{2,1,0:T(8,128)(2,1)S(1)}, u32[]{:S(2)}, u32[]{:S(2)}) %collective-permute-start.1) | collective-permute-done | bytes 1572896 | tf_op jit(solution)/shard_map/ppermute | solution.py:15
  24.5 0.0 copy-done
  24.5 0.6 fusion.24
  25.1 0.0 collective-permute-done.2
  25.1 0.0 copy-done.1
  25.1 1.1 fusion.42
  26.3 31.8 %collective-permute-start.4 = (bf16[6,512,256]{2,1,0:T(8,128)(2,1)S(1)}, bf16[6,512,256]{2,1,0:T(8,128)(2,1)S(1)}, u32[]{:S(2)}, u32[]{:S(2)}) collective-permute-start(bf16[6,512,256]{2,1,0:T(8,128)(2,1)S(1)} %get-tuple-element.5), channel_id=1, source_target_pairs={{0,1},{1,2},{2,3},{3,4},{4,5},{5,6},{6,7},{7,8},{8,9},{9,10},{10,1... | collective-permute-start | bytes 4718600 | tf_op jit(solution)/shard_map/ppermute | solution.py:15
  58.0 0.0 collective-permute-start.3
  58.0 3.5 %collective-permute-start.5 = (bf16[6,512,256]{2,1,0:T(8,128)(2,1)S(1)}, bf16[6,512,256]{2,1,0:T(8,128)(2,1)S(1)}, u32[]{:S(2)}, u32[]{:S(2)}) collective-permute-start(bf16[6,512,256]{2,1,0:T(8,128)(2,1)S(1)} %get-tuple-element.5), channel_id=1, source_target_pairs={{0,15},{1,0},{2,1},{3,2},{4,3},{5,4},{6,5},{7,6},{8,7},{9,8},{10,9... | collective-permute-start | bytes 4718600 | tf_op jit(solution)/shard_map/ppermute | solution.py:15
  61.6 0.6 fusion.18
  62.2 0.0 collective-permute-done.4
  62.2 0.6 fusion.14
  62.7 46.9 %collective-permute-done.3 = bf16[6,512,256]{2,1,0:T(8,128)(2,1)S(1)} collective-permute-done((bf16[6,512,256]{2,1,0:T(8,128)(2,1)S(1)}, bf16[6,512,256]{2,1,0:T(8,128)(2,1)S(1)}, u32[]{:S(2)}, u32[]{:S(2)}) %collective-permute-start.3) | collective-permute-done | bytes 1572896 | tf_op jit(solution)/shard_map/ppermute | solution.py:10
  109.6 0.6 fusion.16
  110.2 0.0 collective-permute-done.5
  110.2 1.1 fusion.43
  111.3 16.4 %collective-permute-start.7 = (bf16[6,512,256]{2,1,0:T(8,128)(2,1)S(1)}, bf16[6,512,256]{2,1,0:T(8,128)(2,1)S(1)}, u32[]{:S(2)}, u32[]{:S(2)}) collective-permute-start(bf16[6,512,256]{2,1,0:T(8,128)(2,1)S(1)} %get-tuple-element.7), channel_id=1, source_target_pairs={{0,1},{1,2},{2,3},{3,4},{4,5},{5,6},{6,7},{7,8},{8,9},{9,10},{10,1... | collective-permute-start | bytes 4718600 | tf_op jit(solution)/shard_map/ppermute | solution.py:15
  127.7 0.7 collective-permute-start.6
  128.3 3.5 %collective-permute-start.8 = (bf16[6,512,256]{2,1,0:T(8,128)(2,1)S(1)}, bf16[6,512,256]{2,1,0:T(8,128)(2,1)S(1)}, u32[]{:S(2)}, u32[]{:S(2)}) collective-permute-start(bf16[6,512,256]{2,1,0:T(8,128)(2,1)S(1)} %get-tuple-element.7), channel_id=1, source_target_pairs={{0,15},{1,0},{2,1},{3,2},{4,3},{5,4},{6,5},{7,6},{8,7},{9,8},{10,9... | collective-permute-start | bytes 4718600 | tf_op jit(solution)/shard_map/ppermute | solution.py:15
  131.8 0.6 fusion.8
  132.4 33.0 %collective-permute-done.7 = bf16[6,512,256]{2,1,0:T(8,128)(2,1)S(1)} collective-permute-done((bf16[6,512,256]{2,1,0:T(8,128)(2,1)S(1)}, bf16[6,512,256]{2,1,0:T(8,128)(2,1)S(1)}, u32[]{:S(2)}, u32[]{:S(2)}) %collective-permute-start.7) | collective-permute-done | bytes 1572896 | tf_op jit(solution)/shard_map/ppermute | solution.py:15
  165.4 0.6 fusion.4
  166.0 0.0 collective-permute-done.6
  166.0 0.6 fusion.6
  166.6 12.5 %collective-permute-done.8 = bf16[6,512,256]{2,1,0:T(8,128)(2,1)S(1)} collective-permute-done((bf16[6,512,256]{2,1,0:T(8,128)(2,1)S(1)}, bf16[6,512,256]{2,1,0:T(8,128)(2,1)S(1)}, u32[]{:S(2)}, u32[]{:S(2)}) %collective-permute-start.8) | collective-permute-done | bytes 1572896 | tf_op jit(solution)/shard_map/ppermute | solution.py:15
  179.1 2.8 %multiply_add_fusion = f32[6,512,256]{2,1,0:T(8,128)} fusion(f32[6,512,256]{2,1,0:T(8,128)S(1)} %get-tuple-element.8, f32[6,512,256]{2,1,0:T(8,128)S(1)} %fusion.4, f32[6,512,256]{2,1,0:T(8,128)S(1)} %fusion.8, f32[6,512,256]{2,1,0:T(8,128)S(1)} %fusion.6, f32[6,256]{1,0:T(8,128)S(1)} %convert_element_type.14, ...), kind=kOutput, calls=%fused_computation | convolution fusion | flops 406585344 | bytes 18096128 | tf_op jit(solution)/shard_map/bnr,brs->bns/dot_general | solution.py:19
Async XLA Ops:
  0.0 9.2 %collective-permute-start = (bf16[6,512,256]{2,1,0:T(8,128)(2,1)}, bf16[6,512,256]{2,1,0:T(8,128)(2,1)S(1)}, u32[]{:S(2)}, u32[]{:S(2)}) collective-permute-start(bf16[6,512,256]{2,1,0:T(8,128)(2,1)} %param.3), channel_id=1, source_target_pairs={{0,1},{1,0},{2,3},{3,2},{4,5},{5,4},{6,7},{7,6},{8,9},{9,8},{10,11... | collective-permute-start | bytes 4718600 | tf_op jit(solution)/shard_map/ppermute | solution.py:10
  0.5 24.1 %collective-permute-start.1 = (bf16[6,512,256]{2,1,0:T(8,128)(2,1)}, bf16[6,512,256]{2,1,0:T(8,128)(2,1)S(1)}, u32[]{:S(2)}, u32[]{:S(2)}) collective-permute-start(bf16[6,512,256]{2,1,0:T(8,128)(2,1)} %param.3), channel_id=1, source_target_pairs={{0,1},{1,2},{2,3},{3,4},{4,5},{5,6},{6,7},{7,8},{8,9},{9,10},{10,1... | collective-permute-start | bytes 4718600 | tf_op jit(solution)/shard_map/ppermute | solution.py:15
  0.5 24.6 %collective-permute-start.2 = (bf16[6,512,256]{2,1,0:T(8,128)(2,1)}, bf16[6,512,256]{2,1,0:T(8,128)(2,1)S(1)}, u32[]{:S(2)}, u32[]{:S(2)}) collective-permute-start(bf16[6,512,256]{2,1,0:T(8,128)(2,1)} %param.3), channel_id=1, source_target_pairs={{0,15},{1,0},{2,1},{3,2},{4,3},{5,4},{6,5},{7,6},{8,7},{9,8},{10,9... | collective-permute-start | bytes 4718600 | tf_op jit(solution)/shard_map/ppermute | solution.py:15
  6.8 17.7 %copy-start = (bf16[4,3,6,256,256]{4,3,2,1,0:T(8,128)(2,1)S(1)}, bf16[4,3,6,256,256]{4,3,2,1,0:T(8,128)(2,1)}, u32[]{:S(2)}) copy-start(bf16[4,3,6,256,256]{4,3,2,1,0:T(8,128)(2,1)} %param.4) | copy-start | bytes 28311556
  11.3 13.8 %copy-start.1 = (bf16[6,512,256]{2,1,0:T(8,128)(2,1)S(1)}, bf16[6,512,256]{2,1,0:T(8,128)(2,1)}, u32[]{:S(2)}) copy-start(bf16[6,512,256]{2,1,0:T(8,128)(2,1)} %param.3) | copy-start | bytes 4718596
  26.3 35.9 %collective-permute-start.4 = (bf16[6,512,256]{2,1,0:T(8,128)(2,1)S(1)}, bf16[6,512,256]{2,1,0:T(8,128)(2,1)S(1)}, u32[]{:S(2)}, u32[]{:S(2)}) collective-permute-start(bf16[6,512,256]{2,1,0:T(8,128)(2,1)S(1)} %get-tuple-element.5), channel_id=1, source_target_pairs={{0,1},{1,2},{2,3},{3,4},{4,5},{5,6},{6,7},{7,8},{8,9},{9,10},{10,1... | collective-permute-start | bytes 4718600 | tf_op jit(solution)/shard_map/ppermute | solution.py:15
  58.0 51.6 %collective-permute-start.3 = (bf16[6,512,256]{2,1,0:T(8,128)(2,1)S(1)}, bf16[6,512,256]{2,1,0:T(8,128)(2,1)S(1)}, u32[]{:S(2)}, u32[]{:S(2)}) collective-permute-start(bf16[6,512,256]{2,1,0:T(8,128)(2,1)S(1)} %get-tuple-element.5), channel_id=1, source_target_pairs={{0,2},{1,3},{2,0},{3,1},{4,6},{5,7},{6,4},{7,5},{8,10},{9,11},{10,... | collective-permute-start | bytes 4718600 | tf_op jit(solution)/shard_map/ppermute | solution.py:10
  58.0 52.2 %collective-permute-start.5 = (bf16[6,512,256]{2,1,0:T(8,128)(2,1)S(1)}, bf16[6,512,256]{2,1,0:T(8,128)(2,1)S(1)}, u32[]{:S(2)}, u32[]{:S(2)}) collective-permute-start(bf16[6,512,256]{2,1,0:T(8,128)(2,1)S(1)} %get-tuple-element.5), channel_id=1, source_target_pairs={{0,15},{1,0},{2,1},{3,2},{4,3},{5,4},{6,5},{7,6},{8,7},{9,8},{10,9... | collective-permute-start | bytes 4718600 | tf_op jit(solution)/shard_map/ppermute | solution.py:15
  111.3 54.1 %collective-permute-start.7 = (bf16[6,512,256]{2,1,0:T(8,128)(2,1)S(1)}, bf16[6,512,256]{2,1,0:T(8,128)(2,1)S(1)}, u32[]{:S(2)}, u32[]{:S(2)}) collective-permute-start(bf16[6,512,256]{2,1,0:T(8,128)(2,1)S(1)} %get-tuple-element.7), channel_id=1, source_target_pairs={{0,1},{1,2},{2,3},{3,4},{4,5},{5,6},{6,7},{7,8},{8,9},{9,10},{10,1... | collective-permute-start | bytes 4718600 | tf_op jit(solution)/shard_map/ppermute | solution.py:15
  127.7 38.3 %collective-permute-start.6 = (bf16[6,512,256]{2,1,0:T(8,128)(2,1)S(1)}, bf16[6,512,256]{2,1,0:T(8,128)(2,1)S(1)}, u32[]{:S(2)}, u32[]{:S(2)}) collective-permute-start(bf16[6,512,256]{2,1,0:T(8,128)(2,1)S(1)} %get-tuple-element.7), channel_id=1, source_target_pairs={{0,4},{1,5},{2,6},{3,7},{4,0},{5,1},{6,2},{7,3},{8,12},{9,13},{10,... | collective-permute-start | bytes 4718600 | tf_op jit(solution)/shard_map/ppermute | solution.py:10
  128.3 50.7 %collective-permute-start.8 = (bf16[6,512,256]{2,1,0:T(8,128)(2,1)S(1)}, bf16[6,512,256]{2,1,0:T(8,128)(2,1)S(1)}, u32[]{:S(2)}, u32[]{:S(2)}) collective-permute-start(bf16[6,512,256]{2,1,0:T(8,128)(2,1)S(1)} %get-tuple-element.7), channel_id=1, source_target_pairs={{0,15},{1,0},{2,1},{3,2},{4,3},{5,4},{6,5},{7,6},{8,7},{9,8},{10,9... | collective-permute-start | bytes 4718600 | tf_op jit(solution)/shard_map/ppermute | solution.py:15
where the time goes:
time: 184 us; the launch traced here: 182 us
  waiting for transfers between devices  106 us (58%)
  starting transfers between devices  62 us (34%)
  matrix products  13.5 us (7%)
    ppermute x6, starting transfers between devices, passed_along(): return lax.ppermute(x, axis, [(i, (i + by) % count) for i in range(count)])  60.9 us
    ppermute x6, waiting for transfers between devices, passed_along(): return lax.ppermute(x, axis, [(i, (i + by) % count) for i in range(count)])  58.7 us
    ppermute x3, waiting for transfers between devices, from_partner(): lax.ppermute(x, axis, [(i, i ^ 1 << stride) for i in range(lax.axis_size(...  46.9 us
    dot_general x12, matrix products, product(): jnp.einsum('bnr,brs->bns', source, weight, preferred_element_type=jnp.flo...  13.5 us
  transfers between devices with their start and end apart: 9, of which 4 were waited for; matrix products, arithmetic and copies ran while one was open for 5% of the time, Pallas kernels for 0%

commit v1 on v0

v1 whole, which is shorter than its diff:
```python
import functools

import jax
import jax.numpy as jnp
from jax import lax
from jax.experimental import pallas as pl
from jax.experimental.pallas import tpu as pltpu
from jax.sharding import PartitionSpec as P

LEVELS = 3
SPLIT = 2
LAG = 2
LEAD = 3

PAIR, RING, PARTNER = range(3)


def kernel(count, pieces, rhs, tiles, occ, out, weights, state, sent, pair, ring, partner,
           send_sem, recv_sem, rhs_sem, tile_sem, out_sem):
    me = lax.axis_index("bx")
    boxes = pieces // SPLIT
    even = lax.rem(me, 2) == 0
    inner = (lax.rem(me, 4) == 1) | (lax.rem(me, 4) == 2)

    def flipped(by):
        return jnp.where(lax.rem(me // by, 2) == 0, me + by, me - by)

    def along(by):
        return lax.rem(me + jnp.where(even, count - by, by), count)

    mate, across, beyond = flipped(1), flipped(2), flipped(4)
    neighbour, far = along(1), along(3)
    relay = jnp.where(inner, far, mate)
    mate_tile = jnp.where(even, 3, 2)

    def rhs_copy(i):
        return pltpu.make_async_copy(rhs.at[i], sent.at[0, i], rhs_sem.at[i])

    def tile_copy(level, k):
        return pltpu.make_async_copy(tiles.at[:, level, k], weights.at[level, k], tile_sem.at[level, k])

    def out_copy(i):
        return pltpu.make_async_copy(state.at[i], out.at[i], out_sem.at[i])

    def remote(level, kind, i):
        source = sent.at[level, i]
        if kind == PAIR:
            target, device = pair.at[level, i], mate
        elif kind == PARTNER:
            target, device = partner.at[level - 1, i], across if level == 1 else beyond
        else:
            target, device = ring.at[level, i], neighbour
            if level == 1:
                source, device = partner.at[0, i], relay
        return pltpu.make_async_remote_copy(
            src_ref=source,
            dst_ref=target,
            send_sem=send_sem.at[level, kind, i],
            recv_sem=recv_sem.at[level, kind, i],
            device_id={"bx": device},
            device_id_type=pl.DeviceIdType.MESH,
        )

    def send(level, i):
        if level > 0:
            remote(level, PARTNER, i).start()
        if level != 1:
            remote(level, RING, i).start()
        remote(level, PAIR, i).start()

    def forward(i):
        remote(1, PARTNER, i).wait_recv()
        remote(1, RING, i).start()

    def work(level, i):
        k = i // SPLIT

        @pl.when(lax.rem(i, SPLIT) == 0)
        def _():
            tile_copy(level, k).wait()

        remote(level, PAIR, i).wait_recv()
        remote(level, RING, i).wait_recv()
        if level == 2:
            remote(level, PARTNER, i).wait_recv()

        def product(source, kind):
            return jnp.dot(source, weights[level, k, kind], preferred_element_type=jnp.float32)

        own, beside = sent[level, i], pair[level, i]
        met = beside if level == 0 else partner[level - 1, i]
        coupled = product(own, 0) + product(met, 1)
        coupled = coupled + product(beside, mate_tile) + product(ring[level, i], 5 - mate_tile)
        keep = occ[pl.ds(k, 1), :].astype(jnp.float32)
        before = own.astype(jnp.float32) if level == 0 else state[i]
        after = before + keep * coupled
        state[i] = after
        if level < LEVELS - 1:
            sent[level + 1, i] = after.astype(jnp.bfloat16)
            send(level + 1, i)
        else:
            out_copy(i).start()

    def each(start, stop, step):
        def run(i, carry):
            step(i)
            return carry

        lax.fori_loop(start, stop, run, 0)

    each(0, pieces, lambda i: rhs_copy(i).start())
    barrier = pltpu.get_barrier_semaphore()
    for other in (mate, across, beyond, neighbour, far):
        pl.semaphore_signal(barrier, inc=1, device_id={"bx": other}, device_id_type=pl.DeviceIdType.MESH)
    for level in range(LEVELS):
        each(0, boxes, lambda k: tile_copy(level, k).start())
    each(0, pieces, lambda i: rhs_copy(i).wait())
    pl.semaphore_wait(barrier, 5)
    each(0, LEAD, lambda i: send(0, i))

    def step(s):
        def when_valid(i, action):
            @pl.when((i >= 0) & (i < pieces))
            def _():
                action(i)

        when_valid(s, lambda i: work(0, i))
        when_valid(s + LEAD, lambda i: send(0, i))
        when_valid(s - LAG + 1, forward)
        when_valid(s - LAG, lambda i: work(1, i))
        when_valid(s - 2 * LAG, lambda i: work(2, i))

    each(0, pieces + 2 * LAG, step)

    def finish(i):
        for level in range(LEVELS):
            for kind in (PAIR, RING, PARTNER):
                if level or kind != PARTNER:
                    remote(level, kind, i).wait_send()
        out_copy(i).wait()

    each(0, pieces, finish)


def body(count, rhs, tiles, occupancy):
    boxes, columns, rows = rhs.shape
    pieces, part = boxes * SPLIT, columns // SPLIT
    block = (pieces, part, rows)
    out = pl.pallas_call(
        functools.partial(kernel, count, pieces),
        out_shape=jax.ShapeDtypeStruct(block, jnp.float32),
        in_specs=[
            pl.BlockSpec(memory_space=pl.ANY),
            pl.BlockSpec(memory_space=pl.ANY),
            pl.BlockSpec(memory_space=pltpu.VMEM),
        ],
        out_specs=pl.BlockSpec(memory_space=pl.ANY),
        scratch_shapes=[
            pltpu.VMEM((LEVELS, boxes, 4, rows, rows), jnp.bfloat16),
            pltpu.VMEM(block, jnp.float32),
            pltpu.VMEM((LEVELS, *block), jnp.bfloat16),
            pltpu.VMEM((LEVELS, *block), jnp.bfloat16),
            pltpu.VMEM((LEVELS, *block), jnp.bfloat16),
            pltpu.VMEM((LEVELS - 1, *block), jnp.bfloat16),
            pltpu.SemaphoreType.DMA((LEVELS, 3, pieces)),
            pltpu.SemaphoreType.DMA((LEVELS, 3, pieces)),
            pltpu.SemaphoreType.DMA((pieces,)),
            pltpu.SemaphoreType.DMA((LEVELS, boxes)),
            pltpu.SemaphoreType.DMA((pieces,)),
        ],
        compiler_params=pltpu.CompilerParams(
            collective_id=0, has_side_effects=True, vmem_limit_bytes=56 << 20
        ),
        cost_estimate=pl.CostEstimate(
            flops=8 * LEVELS * boxes * columns * rows * rows,
            bytes_accessed=2 * tiles.size + 6 * rhs.size,
            transcendentals=0,
        ),
    )(rhs.reshape(block), tiles, occupancy)
    return out.reshape(boxes, columns, rows)


def solution(mesh):
    placed = (
        P(("groups", "bx"), None, None),
        P(None, None, ("groups", "bx"), None, None),
        P(("groups", "bx"), None),
    )
    return jax.shard_map(
        functools.partial(body, mesh.shape["bx"]),
        mesh=mesh,
        in_specs=placed,
        out_specs=P(("groups", "bx"), None, None),
        check_vma=False,
    )
```

time: 184 us -> 121 us (0.66)
  Pallas kernels: 0 us -> 117 us
  waiting for transfers between devices: 106 us -> 0 us
  starting transfers between devices: 62 us -> 0 us
  matrix products: 13.5 us -> 0 us
  local copies, waits for them, and re-layouts: 0.01 us -> 3.94 us
    pallas_call x0 -> x1, Pallas kernels: none -> 117 us  [body(): pl.pallas_call(functools.partial(kernel, count, pieces), out_shape=jax.Sh...]
    ppermute x9 -> x0, waiting for transfers between devices: 106 us -> none  [the longest x6 58.7 us: passed_along(): return lax.ppermute(x, axis, [(i, (i + by) % count) for i in range(count)])]
    ppermute x9 -> x0, starting transfers between devices: 62 us -> none  [the longest x6 60.9 us: passed_along(): return lax.ppermute(x, axis, [(i, (i + by) % count) for i in range(count)])]
    dot_general x12 -> x0, matrix products: 13.5 us -> none  [product(): jnp.einsum('bnr,brs->bns', source, weight, preferred_element_type=jnp.flo...]
    unnamed x4 -> x1, local copies, waits for them, and re-layouts: 0.01 us -> 3.94 us
  transfers between devices with their start and end apart: 9 -> 0, of which waited for: 4 -> 0; matrix products, arithmetic and copies ran while one was open for 5% -> 0% of each run, Pallas kernels for 0% -> 0%
where the time goes in v1:
time: 121 us
  Pallas kernels  117 us (97%)
  local copies, waits for them, and re-layouts  3.94 us (3%)
    pallas_call x1, Pallas kernels, body(): pl.pallas_call(functools.partial(kernel, count, pieces), out_shape=jax.Sh...  117 us
    unnamed x1, local copies, waits for them, and re-layouts  3.94 us

profile of v1, /device:TPU:0, one launch (start us, length us, event | category | flops | bytes accessed | tf_op | source)
XLA Modules:
  0.0 120.6 jit_solution(10987481651526996779)
XLA Ops:
  0.0 116.7 %shard_map.37 = f32[12,256,256]{2,1,0:T(8,128)} custom-call(bf16[12,256,256]{2,1,0:T(8,128)(2,1)} %bitcast.3, bf16[4,3,6,256,256]{4,3,2,1,0:T(8,128)(2,1)} %tiles.1, s32[6,256]{1,0:T(8,128)} %occ.1), custom_call_target="tpu_custom_call" | custom-call | flops 4831838208 | bytes 14155776 | tf_op jit(solution)/shard_map/pallas_call | solution.py:149
  116.7 3.9 %copy.5 = f32[6,512,256]{2,1,0:T(8,128)} copy(f32[6,512,256]{2,1,0:T(8,128)} %bitcast.2) | data formatting | bytes 6291456

commit v2 on v1

--- a/solution.py
+++ b/solution.py
@@ -10,13 +10,13 @@
 LEVELS = 3
 SPLIT = 2
 LAG = 2
-LEAD = 3
+LEAD = 2
 
 PAIR, RING, PARTNER = range(3)
 
 
-def kernel(count, pieces, rhs, tiles, occ, out, weights, state, sent, pair, ring, partner,
-           send_sem, recv_sem, rhs_sem, tile_sem, out_sem):
+def kernel(count, pieces, rhs, tiles, occ, state, weights, sent, pair, ring, partner,
+           send_sem, recv_sem, rhs_sem, tile_sem):
     me = lax.axis_index("bx")
     boxes = pieces // SPLIT
     even = lax.rem(me, 2) == 0
@@ -38,9 +38,6 @@
 
     def tile_copy(level, k):
         return pltpu.make_async_copy(tiles.at[:, level, k], weights.at[level, k], tile_sem.at[level, k])
-
-    def out_copy(i):
-        return pltpu.make_async_copy(state.at[i], out.at[i], out_sem.at[i])
 
     def remote(level, kind, i):
         source = sent.at[level, i]
@@ -98,8 +95,6 @@
         if level < LEVELS - 1:
             sent[level + 1, i] = after.astype(jnp.bfloat16)
             send(level + 1, i)
-        else:
-            out_copy(i).start()
 
     def each(start, stop, step):
         def run(i, carry):
@@ -137,7 +132,6 @@
             for kind in (PAIR, RING, PARTNER):
                 if level or kind != PARTNER:
                     remote(level, kind, i).wait_send()
-        out_copy(i).wait()
 
     each(0, pieces, finish)
 
@@ -148,16 +142,15 @@
     block = (pieces, part, rows)
     out = pl.pallas_call(
         functools.partial(kernel, count, pieces),
-        out_shape=jax.ShapeDtypeStruct(block, jnp.float32),
+        out_shape=pltpu.VMEM(block, jnp.float32),
         in_specs=[
             pl.BlockSpec(memory_space=pl.ANY),
             pl.BlockSpec(memory_space=pl.ANY),
             pl.BlockSpec(memory_space=pltpu.VMEM),
         ],
-        out_specs=pl.BlockSpec(memory_space=pl.ANY),
+        out_specs=pl.BlockSpec(memory_space=pltpu.VMEM),
         scratch_shapes=[
             pltpu.VMEM((LEVELS, boxes, 4, rows, rows), jnp.bfloat16),
-            pltpu.VMEM(block, jnp.float32),
             pltpu.VMEM((LEVELS, *block), jnp.bfloat16),
             pltpu.VMEM((LEVELS, *block), jnp.bfloat16),
             pltpu.VMEM((LEVELS, *block), jnp.bfloat16),
@@ -166,7 +159,6 @@
             pltpu.SemaphoreType.DMA((LEVELS, 3, pieces)),
             pltpu.SemaphoreType.DMA((pieces,)),
             pltpu.SemaphoreType.DMA((LEVELS, boxes)),
-            pltpu.SemaphoreType.DMA((pieces,)),
         ],
         compiler_params=pltpu.CompilerParams(
             collective_id=0, has_side_effects=True, vmem_limit_bytes=56 << 20

time: 121 us -> 117 us (0.967)
  local copies, waits for them, and re-layouts: 3.94 us -> 1.67 us
  Pallas kernels: 117 us -> 115 us
    unnamed x1, local copies, waits for them, and re-layouts: 3.94 us -> 1.67 us
    pallas_call x1, Pallas kernels: 117 us -> 115 us  [body(): pl.pallas_call(functools.partial(kernel, count, pieces), out_shape=pltpu....]
where the time goes in v2:
time: 117 us; the launch traced here: 116 us
  Pallas kernels  115 us (98%)
  local copies, waits for them, and re-layouts  1.67 us (1%)
    pallas_call x1, Pallas kernels, body(): pl.pallas_call(functools.partial(kernel, count, pieces), out_shape=pltpu....  115 us

profile of v2, /device:TPU:0, one launch (start us, length us, event | category | flops | bytes accessed | tf_op | source)
XLA Modules:
  0.0 116.5 jit_solution(11459472531004132548)
XLA Ops:
  0.0 114.8 %shard_map.37 = f32[12,256,256]{2,1,0:T(8,128)S(1)} custom-call(bf16[12,256,256]{2,1,0:T(8,128)(2,1)} %bitcast.3, bf16[4,3,6,256,256]{4,3,2,1,0:T(8,128)(2,1)} %tiles.1, s32[6,256]{1,0:T(8,128)} %occ.1), custom_call_target="tpu_custom_call" | custom-call | flops 4831838208 | bytes 14155776 | tf_op jit(solution)/shard_map/pallas_call | solution.py:143
  114.8 1.7 %copy.5 = f32[6,512,256]{2,1,0:T(8,128)} copy(f32[6,512,256]{2,1,0:T(8,128)S(1)} %bitcast.2) | data formatting | bytes 6291456

commit v3 on v2

--- a/solution.py
+++ b/solution.py
@@ -9,7 +9,9 @@
 
 LEVELS = 3
 SPLIT = 2
-LAG = 2
+LAG_MIDDLE = 2
+LAG_LAST = 7
+RELAY = 1
 LEAD = 2
 
 PAIR, RING, PARTNER = range(3)
@@ -103,10 +105,10 @@
 
         lax.fori_loop(start, stop, run, 0)
 
+    barrier = pltpu.get_barrier_semaphore()
+    for other in (far, neighbour, beyond, across, mate):
+        pl.semaphore_signal(barrier, inc=1, device_id={"bx": other}, device_id_type=pl.DeviceIdType.MESH)
     each(0, pieces, lambda i: rhs_copy(i).start())
-    barrier = pltpu.get_barrier_semaphore()
-    for other in (mate, across, beyond, neighbour, far):
-        pl.semaphore_signal(barrier, inc=1, device_id={"bx": other}, device_id_type=pl.DeviceIdType.MESH)
     for level in range(LEVELS):
         each(0, boxes, lambda k: tile_copy(level, k).start())
     each(0, pieces, lambda i: rhs_copy(i).wait())
@@ -121,11 +123,11 @@
 
         when_valid(s, lambda i: work(0, i))
         when_valid(s + LEAD, lambda i: send(0, i))
-        when_valid(s - LAG + 1, forward)
-        when_valid(s - LAG, lambda i: work(1, i))
-        when_valid(s - 2 * LAG, lambda i: work(2, i))
+        when_valid(s - RELAY, forward)
+        when_valid(s - LAG_MIDDLE, lambda i: work(1, i))
+        when_valid(s - LAG_LAST, lambda i: work(2, i))
 
-    each(0, pieces + 2 * LAG, step)
+    each(0, pieces + LAG_LAST, step)
 
     def finish(i):
         for level in range(LEVELS):

time: 117 us -> 116 us (level)
  no operation moved by 1% of the time
where the time goes in v3:
time: 116 us
  Pallas kernels  114 us (98%)
  local copies, waits for them, and re-layouts  1.67 us (1%)
    pallas_call x1, Pallas kernels, body(): pl.pallas_call(functools.partial(kernel, count, pieces), out_shape=pltpu....  114 us

profile of v3, /device:TPU:0, one launch (start us, length us, event | category | flops | bytes accessed | tf_op | source)
XLA Modules:
  0.0 116.1 jit_solution(5348996814758678833)
XLA Ops:
  0.0 114.5 %shard_map.37 = f32[12,256,256]{2,1,0:T(8,128)S(1)} custom-call(bf16[12,256,256]{2,1,0:T(8,128)(2,1)} %bitcast.3, bf16[4,3,6,256,256]{4,3,2,1,0:T(8,128)(2,1)} %tiles.1, s32[6,256]{1,0:T(8,128)} %occ.1), custom_call_target="tpu_custom_call" | custom-call | flops 4831838208 | bytes 14155776 | tf_op jit(solution)/shard_map/pallas_call | solution.py:145
  114.5 1.7 %copy.5 = f32[6,512,256]{2,1,0:T(8,128)} copy(f32[6,512,256]{2,1,0:T(8,128)S(1)} %bitcast.2) | data formatting | bytes 6291456

commit v4 on v3

--- a/solution.py
+++ b/solution.py
@@ -98,6 +98,12 @@
             sent[level + 1, i] = after.astype(jnp.bfloat16)
             send(level + 1, i)
 
+    def finish(i):
+        for level in range(LEVELS):
+            for kind in (PAIR, RING, PARTNER):
+                if level or kind != PARTNER:
+                    remote(level, kind, i).wait_send()
+
     def each(start, stop, step):
         def run(i, carry):
             step(i)
@@ -125,17 +131,10 @@
         when_valid(s + LEAD, lambda i: send(0, i))
         when_valid(s - RELAY, forward)
         when_valid(s - LAG_MIDDLE, lambda i: work(1, i))
+        when_valid(s - LAG_LAST, finish)
         when_valid(s - LAG_LAST, lambda i: work(2, i))
 
     each(0, pieces + LAG_LAST, step)
-
-    def finish(i):
-        for level in range(LEVELS):
-            for kind in (PAIR, RING, PARTNER):
-                if level or kind != PARTNER:
-                    remote(level, kind, i).wait_send()
-
-    each(0, pieces, finish)
 
 
 def body(count, rhs, tiles, occupancy):

time: 116 us -> 117 us (level)
  no operation moved by 1% of the time
where the time goes in v4:
time: 117 us; the launch traced here: 116 us
  Pallas kernels  115 us (98%)
  local copies, waits for them, and re-layouts  1.67 us (1%)
    pallas_call x1, Pallas kernels, body(): pl.pallas_call(functools.partial(kernel, count, pieces), out_shape=pltpu....  115 us

profile of v4, /device:TPU:0, one launch (start us, length us, event | category | flops | bytes accessed | tf_op | source)
XLA Modules:
  0.0 116.3 jit_solution(2905777384768931809)
XLA Ops:
  0.0 114.7 %shard_map.37 = f32[12,256,256]{2,1,0:T(8,128)S(1)} custom-call(bf16[12,256,256]{2,1,0:T(8,128)(2,1)} %bitcast.3, bf16[4,3,6,256,256]{4,3,2,1,0:T(8,128)(2,1)} %tiles.1, s32[6,256]{1,0:T(8,128)} %occ.1), custom_call_target="tpu_custom_call" | custom-call | flops 4831838208 | bytes 14155776 | tf_op jit(solution)/shard_map/pallas_call | solution.py:144
  114.7 1.7 %copy.5 = f32[6,512,256]{2,1,0:T(8,128)} copy(f32[6,512,256]{2,1,0:T(8,128)S(1)} %bitcast.2) | data formatting | bytes 6291456
